TPU v7x, 32 devices: a whole 2x2x4 slice. The times are simulated.
32 devices in a mesh: shot: 8 (over z, x), az: 4 (over y, core).
Axes of the slice: x: 2, y: 2, z: 4, core: 2. Of those that a mesh axis runs over, the one named last changes fastest.
Arguments:
- spectra: bfloat16 [4, 32, 4096, 128], P('az', None, 'shot'), may hold values from -6 to 6
- sampled_mask: int32 [4, 32, 16, 256], P('az', 'shot'), may hold values 0 or 1
- counts: int32 [4, 32], P('az', 'shot'), may hold values from 1 to 6, as said below
Outputs:
- blended: bfloat16 [4, 32, 2048, 128], P('az', None, 'shot')
Inputs may be any that keep to these rules, and one draw needn't show every extreme that they name: `counts`: every draw holds a patch with 1 iteration and a patch with 6.
All inputs are finite; a program needn't handle non-finite values. No bound on the sum of `sampled_mask` on one device may be relied on, other than what follows from the above.
Results may differ from a plain program's by a relative error of at most 0.008.
Values may be sent and summed in bfloat16 or wider, within the bound.
A program may use at most 64 MiB of HBM per device.

v0:
```python
import jax
import jax.numpy as jnp
from jax import lax
from jax.sharding import PartitionSpec as P


def passed_along(block, axis, distance):
    devices = range(lax.axis_size(axis))
    route = [(i - distance, i) for i in devices if i - distance in devices]
    return lax.ppermute(block, axis, route)


def dft_tables(extent):
    indices = jnp.arange(extent, dtype=jnp.int32)
    product = indices[:, None] * indices[None, :] % extent
    phase = product.astype(jnp.float32) * (2.0 * jnp.pi / extent)
    scale = extent ** (-0.5)
    cos_table = jnp.cos(phase) * scale
    sin_table = -jnp.sin(phase) * scale
    kron_real = jnp.kron(cos_table, cos_table) - jnp.kron(sin_table, sin_table)
    kron_imag = jnp.kron(cos_table, sin_table) + jnp.kron(sin_table, cos_table)
    return (
        cos_table.astype(jnp.bfloat16),
        sin_table.astype(jnp.bfloat16),
        kron_real.astype(jnp.bfloat16),
        kron_imag.astype(jnp.bfloat16),
    )


def apply_along(mat_real, mat_imag, volume, pattern):
    halfway = volume.shape[-1] // 2
    rotated = jnp.concatenate([-volume[..., halfway:], volume[..., :halfway]], axis=-1)
    first_part = jnp.einsum(pattern, mat_real, volume, preferred_element_type=jnp.float32)
    second_part = jnp.einsum(pattern, mat_imag, rotated, preferred_element_type=jnp.float32)
    return first_part + second_part


def project_patch(observed, mask_item, sweeps, tables):
    cos_table, sin_table, kron_real, kron_imag = tables
    sampled = (mask_item > 0)[:, :, None]
    initial = jnp.where(sampled, observed, jnp.zeros_like(observed))
    halfway = observed.shape[-1] // 2

    def forward(volume):
        middle = apply_along(kron_real, kron_imag, volume, "kj,ajl->akl").astype(jnp.bfloat16)
        return apply_along(cos_table, sin_table, middle, "ka,ajl->kjl")

    def inverse(volume):
        middle = apply_along(cos_table, -sin_table, volume, "ka,ajl->kjl").astype(jnp.bfloat16)
        return apply_along(kron_real, -kron_imag, middle, "kj,ajl->akl")

    def magnitude(coeffs):
        return jnp.sqrt(coeffs[..., :halfway] ** 2 + coeffs[..., halfway:] ** 2)

    largest = jnp.max(magnitude(forward(initial)), axis=(0, 1))

    def sweep_step(sweep, volume):
        coeffs = forward(volume)
        size_now = magnitude(coeffs)
        cutoff = largest * (0.5 * jnp.power(jnp.float32(0.6), sweep.astype(jnp.float32)))
        factor = jax.nn.relu(size_now - cutoff) / (jnp.maximum(size_now, cutoff) + 1e-06)
        thinned = (coeffs * jnp.concatenate([factor, factor], axis=-1)).astype(jnp.bfloat16)
        returned = inverse(thinned)
        return jnp.where(sampled, observed.astype(jnp.float32), returned).astype(jnp.bfloat16)

    return lax.fori_loop(0, sweeps, sweep_step, initial)


def shards(spectra, sampled_mask, counts):
    regrouped = lax.all_to_all(spectra, "shot", split_axis=1, concat_axis=2, tiled=True)
    owned_count = regrouped.shape[1]
    extent = sampled_mask.shape[2]
    plane = extent * extent
    lane_count = regrouped.shape[3]
    tables = dft_tables(extent)
    observed = regrouped.reshape(owned_count, extent, plane, lane_count)
    masks = sampled_mask[0]
    sweeps = counts[0]

    def run_patch(item):
        return project_patch(item[0], item[1], item[2], tables)

    result = lax.map(run_patch, (observed, masks, sweeps))
    halfway = extent // 2
    arrived = passed_along(result[-1, halfway:], "shot", 1)
    earlier = jnp.concatenate([arrived[None], result[:-1, halfway:]], axis=0).astype(jnp.float32)
    weight = ((jnp.arange(halfway, dtype=jnp.float32) + 0.5) / halfway)[:, None, None]
    mixed = weight * result[:, :halfway].astype(jnp.float32) + (1.0 - weight) * earlier
    mixed = mixed.astype(jnp.bfloat16).reshape(1, owned_count, halfway * plane, lane_count)
    return lax.all_to_all(mixed, "shot", split_axis=2, concat_axis=1, tiled=True)


def solution(mesh):
    return jax.shard_map(
        shards,
        mesh=mesh,
        in_specs=(P("az", None, "shot", None), P("az", "shot", None, None), P("az", "shot")),
        out_specs=P("az", None, "shot", None),
        check_vma=False,
    )
```

profile of v0, /device:TPU:0, one launch (start us, length us, event | category | flops | bytes accessed | tf_op | source)
XLA Modules:
  0.0 644.7 jit_solution(10149699070906165820)
XLA Ops:
  0.0 7.3 %all-to-all-start = ((bf16[1,32,512,128]{3,2,0,1:T(8,128)(2,1)}), bf16[1,32,512,128]{3,2,0,1:T(8,128)(2,1)}, u32[]{:S(2)}, u32[]{:S(2)}) async-start(bf16[1,32,512,128]{3,2,0,1:T(8,128)(2,1)} %bitcast.152), calls=%async_computation | async-start | bytes 8388608 | tf_op jit(solution)/shard_map/all_to_all | solution.py:70
  7.3 93.2 %all-to-all-done = bf16[1,32,512,128]{3,2,0,1:T(8,128)(2,1)} async-done(((bf16[1,32,512,128]{3,2,0,1:T(8,128)(2,1)}), bf16[1,32,512,128]{3,2,0,1:T(8,128)(2,1)}, u32[]{:S(2)}, u32[]{:S(2)}) %all-to-all-start) | async-done | bytes 4194336 | tf_op jit(solution)/shard_map/all_to_all | solution.py:70
  100.5 4.6 copy.39
  105.1 486.9 %while.32 = (s32[]{:T(128)}, bf16[4,16,256,128]{3,2,1,0:T(8,128)(2,1)}, s32[4,16,256]{2,1,0:T(8,128)}, bf16[4,16,256,128]{3,2,1,0:T(8,128)(2,1)}, s32[4]{0:T(128...) while((s32[]{:T(128)}, ...), condition=%wide.region_4.5_spmd.clone.clone.clone, body=%wide.region_0.4_spmd.clone.clone.clone.sunk | while | flops 1737582592 | bytes 113581320 | solution.py:83
  110.8 2.2 convert_element_type.288
  114.0 2.2 reshape.153
  116.3 1.8 fusion.135
  121.1 1.8 copy.63
  122.9 3.0 fusion.137
  127.1 1.9 copy.64
  129.1 2.1 add_bitcast_fusion.4
  132.7 92.3 %while.33 = (s32[]{:T(128)}, bf16[16,256,128]{1,2,0:T(8,128)(2,1)S(1)}, s32[]{:T(128)}, pred[16,256,1]{1,0,2:T(8,128)(4,1)S(1)}, bf16[16,256,128]{1,2,0:T(8,128)...) while((s32[]{:T(128)}, ...), condition=%wide.region_3.3_spmd.clone, body=%wide.region_2.2_spmd.clone.sunk | while | flops 1158676480 | bytes 64494576 | solution.py:66
  139.0 2.0 add_bitcast_fusion.5
  154.3 2.0 add_bitcast_fusion.5
  169.5 2.0 add_bitcast_fusion.5
  184.8 2.0 add_bitcast_fusion.5
  200.1 2.0 add_bitcast_fusion.5
  215.4 2.0 add_bitcast_fusion.5
  232.5 2.2 convert_element_type.288
  235.8 2.2 reshape.153
  238.0 1.8 fusion.135
  242.8 1.8 copy.63
  244.6 3.0 fusion.137
  248.9 1.9 copy.64
  250.8 2.1 add_bitcast_fusion.4
  254.4 92.3 %while.33 = (s32[]{:T(128)}, bf16[16,256,128]{1,2,0:T(8,128)(2,1)S(1)}, s32[]{:T(128)}, pred[16,256,1]{1,0,2:T(8,128)(4,1)S(1)}, bf16[16,256,128]{1,2,0:T(8,128)...) while((s32[]{:T(128)}, ...), condition=%wide.region_3.3_spmd.clone, body=%wide.region_2.2_spmd.clone.sunk | while | flops 1158676480 | bytes 64494576 | solution.py:66
  260.7 2.0 add_bitcast_fusion.5
  276.0 2.0 add_bitcast_fusion.5
  291.3 2.0 add_bitcast_fusion.5
  306.5 2.0 add_bitcast_fusion.5
  321.8 2.0 add_bitcast_fusion.5
  337.1 2.0 add_bitcast_fusion.5
  354.2 2.2 convert_element_type.288
  357.5 2.2 reshape.153
  359.7 1.8 fusion.135
  364.6 1.8 copy.63
  366.4 3.0 fusion.137
  370.6 1.9 copy.64
  372.5 2.1 add_bitcast_fusion.4
  376.2 92.3 %while.33 = (s32[]{:T(128)}, bf16[16,256,128]{1,2,0:T(8,128)(2,1)S(1)}, s32[]{:T(128)}, pred[16,256,1]{1,0,2:T(8,128)(4,1)S(1)}, bf16[16,256,128]{1,2,0:T(8,128)...) while((s32[]{:T(128)}, ...), condition=%wide.region_3.3_spmd.clone, body=%wide.region_2.2_spmd.clone.sunk | while | flops 1158676480 | bytes 64494576 | solution.py:66
  379.4 1.7 fusion.158
  382.4 2.0 add_bitcast_fusion.5
  397.7 2.0 add_bitcast_fusion.5
  413.0 2.0 add_bitcast_fusion.5
  428.3 2.0 add_bitcast_fusion.5
  443.5 2.0 add_bitcast_fusion.5
  458.8 2.0 add_bitcast_fusion.5
  475.9 2.2 convert_element_type.288
  479.2 2.2 reshape.153
  481.4 1.8 fusion.135
  486.3 1.8 copy.63
  488.0 3.0 fusion.137
  492.3 1.9 copy.64
  494.2 2.1 add_bitcast_fusion.4
  497.9 92.3 %while.33 = (s32[]{:T(128)}, bf16[16,256,128]{1,2,0:T(8,128)(2,1)S(1)}, s32[]{:T(128)}, pred[16,256,1]{1,0,2:T(8,128)(4,1)S(1)}, bf16[16,256,128]{1,2,0:T(8,128)...) while((s32[]{:T(128)}, ...), condition=%wide.region_3.3_spmd.clone, body=%wide.region_2.2_spmd.clone.sunk | while | flops 1158676480 | bytes 64494576 | solution.py:66
  504.1 2.0 add_bitcast_fusion.5
  519.4 2.0 add_bitcast_fusion.5
  534.7 2.0 add_bitcast_fusion.5
  550.0 2.0 add_bitcast_fusion.5
  565.2 2.0 add_bitcast_fusion.5
  580.5 2.0 add_bitcast_fusion.5
  596.3 5.1 collective-permute-done
  602.5 9.8 %copy.44 = bf16[1,4,2048,128]{3,1,0,2:T(4,128)(2,1)S(1)} copy(bf16[1,4,2048,128]{3,2,1,0:T(8,128)(2,1)S(1)} %bitcast.150) | data formatting | bytes 4194304 | tf_op jit(solution)/shard_map/reshape | solution.py:89
  612.2 30.7 %all_to_all.33 = bf16[1,4,2048,128]{3,1,0,2:T(4,128)(2,1)S(1)} all-to-all(bf16[1,4,2048,128]{3,1,0,2:T(4,128)(2,1)S(1)} %copy.44), channel_id=1, replica_groups=mesh['shot'=8,'az'=4] {'shot'}, dimensions={2} | all-to-all | bytes 4194304 | tf_op jit(solution)/shard_map/all_to_all | solution.py:90
  (664 shorter events, 361.9 us)
Async XLA Ops:
  0.0 100.5 %all-to-all-start = ((bf16[1,32,512,128]{3,2,0,1:T(8,128)(2,1)}), bf16[1,32,512,128]{3,2,0,1:T(8,128)(2,1)}, u32[]{:S(2)}, u32[]{:S(2)}) async-start(bf16[1,32,512,128]{3,2,0,1:T(8,128)(2,1)} %bitcast.152), calls=%async_computation | async-start | bytes 8388608 | tf_op jit(solution)/shard_map/all_to_all | solution.py:70
  100.5 4.6 copy-start.8
  105.1 4.0 copy-start.4
  105.1 4.0 copy-start.6
  119.0 1.6 copy-start.2
  133.4 1.1 copy-start
  146.1 1.2 copy-start.1
  148.7 1.1 copy-start
  161.4 1.2 copy-start.1
  163.9 1.1 copy-start
  176.6 1.2 copy-start.1
  179.2 1.1 copy-start
  191.9 1.2 copy-start.1
  194.5 1.1 copy-start
  207.2 1.2 copy-start.1
  222.5 1.2 copy-start.1
  225.1 1.8 copy-start.5
  225.1 1.8 copy-start.7
  225.1 1.8 copy-start.9
  226.8 4.0 copy-start.4
  226.9 4.0 copy-start.6
  240.8 1.6 copy-start.2
  255.1 1.1 copy-start
  267.8 1.2 copy-start.1
  270.4 1.1 copy-start
  283.1 1.2 copy-start.1
  298.4 1.2 copy-start.1
  300.9 1.1 copy-start
  313.6 1.2 copy-start.1
  328.9 1.2 copy-start.1
  331.5 1.1 copy-start
  344.2 1.2 copy-start.1
  346.8 1.8 copy-start.5
  346.8 1.8 copy-start.7
  346.8 1.8 copy-start.9
  348.6 4.0 copy-start.4
  348.6 4.0 copy-start.6
  362.5 1.6 copy-start.2
  389.5 1.2 copy-start.1
  392.1 1.1 copy-start
  404.8 1.2 copy-start.1
  407.4 1.1 copy-start
  420.1 1.2 copy-start.1
  422.7 1.1 copy-start
  435.4 1.2 copy-start.1
  450.6 1.2 copy-start.1
  465.9 1.2 copy-start.1
  468.5 1.8 copy-start.5
  468.5 1.8 copy-start.7
  468.5 1.7 copy-start.9
  470.3 4.0 copy-start.4
  470.3 4.0 copy-start.6
  484.2 1.6 copy-start.2
  511.2 1.2 copy-start.1
  526.5 1.2 copy-start.1
  541.8 1.2 copy-start.1
  557.1 1.2 copy-start.1
  572.3 1.2 copy-start.1
  587.6 1.2 copy-start.1
  590.2 1.8 copy-start.5
  590.2 1.8 copy-start.7
  590.2 1.8 copy-start.9
  592.1 9.4 %copy-start.3 = (bf16[4,16,256,128]{3,2,1,0:T(8,128)(2,1)S(1)}, bf16[4,16,256,128]{3,2,1,0:T(8,128)(2,1)}, u32[]{:S(2)}) copy-start(bf16[4,16,256,128]{3,2,1,0:T(8,128)(2,1)} %get-tuple-element.696) | copy-start | bytes 12582916
  593.3 8.1 %collective-permute-start = (bf16[8,256,128]{2,1,0:T(8,128)(2,1)S(1)}, bf16[8,256,128]{2,1,0:T(8,128)(2,1)S(1)}, u32[]{:S(2)}, u32[]{:S(2)}) collective-permute-start(bf16[8,256,128]{2,1,0:T(8,128)(2,1)S(1)} %slice_bitcast_fusion), channel_id=1, source_target_pairs={{0,4},{4,8},{8,12},{12,16},{16,20},{20,24},{24,28},{1,5},{5,9},{9,... | collective-permute-start | bytes 1572872 | tf_op jit(solution)/shard_map/ppermute | solution.py:10
  (12 other events, 12.7 us)
where the time goes:
time: 649 us; the launch traced here: 645 us
  matrix products  198 us (31%)
  local copies, waits for them, and re-layouts  161 us (25%)
  other arithmetic  125 us (19%)
  waiting for transfers between devices  98.3 us (15%)
  blocking collectives  30.7 us (5%)
  loops' own time  22.6 us (3%)
  starting transfers between devices  8.71 us (1%)
    dot_general x104, matrix products, apply_along(): jnp.einsum(pattern, mat_imag, rotated, preferred_element_type=jnp.float32)  104 us
    dot_general x104, matrix products, apply_along(): jnp.einsum(pattern, mat_real, volume, preferred_element_type=jnp.float32)  94 us
    all_to_all x1, waiting for transfers between devices, shards(): lax.all_to_all(spectra, 'shot', split_axis=1, concat_axis=2, tiled=True)  93.2 us
    concatenate x28, local copies, waits for them, and re-layouts, apply_along(): jnp.concatenate([-volume[..., halfway:], volume[..., :halfway]], axis=-1)  33.6 us
    while x144, local copies, waits for them, and re-layouts  33.5 us
    convert_element_type x28, local copies, waits for them, and re-layouts, forward(): apply_along(kron_real, kron_imag, volume, 'kj,ajl->akl')  33.1 us
    all_to_all x1, blocking collectives, shards(): lax.all_to_all(mixed, 'shot', split_axis=2, concat_axis=1, tiled=True)  30.7 us
    div x24, other arithmetic, sweep_step(): jax.nn.relu(size_now - cutoff) / (jnp.maximum(size_now, cutoff) + 1e-06)  28.9 us
  transfers between devices with their start and end apart: 2, of which 2 were waited for; matrix products, arithmetic and copies ran while one was open for 0% of the time, Pallas kernels for 0%

commit v1 on v0

v1 whole, which is shorter than its diff:
```python
import functools

import jax
import jax.numpy as jnp
import ml_dtypes
import numpy as np
from jax import lax
from jax.experimental import pallas as pl
from jax.experimental.pallas import tpu as pltpu
from jax.sharding import PartitionSpec as P


def rounded(table):
    return table.astype(ml_dtypes.bfloat16)


def real_form(real, imag):
    return np.block([[real, -imag], [imag, real]])


def dft_blocks(extent):
    n = np.arange(extent)
    phase = ((n[:, None] * n[None, :]) % extent).astype(np.float32) * np.float32(2.0 * np.pi / extent)
    scale = np.float32(extent ** (-0.5))
    cos = (np.cos(phase) * scale).astype(np.float32)
    sin = (-np.sin(phase) * scale).astype(np.float32)
    kr = np.kron(cos, cos) - np.kron(sin, sin)
    ki = np.kron(cos, sin) + np.kron(sin, cos)
    cos, sin, kr, ki = (rounded(t).astype(np.float32) for t in (cos, sin, kr, ki))
    half, plane = extent // 2, extent * extent
    eye = np.eye(extent, dtype=np.float32)
    ks = lambda t, par: t.reshape(half, 2, extent, plane)[:, par].reshape(plane // 2, plane)[:, : plane // 2]
    out = []
    for par in (0, 1):
        out.append(real_form(ks(kr, par), ks(ki, par)))
    for par in (0, 1):
        out.append(real_form(ks(kr, par).T, -ks(ki, par).T))
    for par in (0, 1):
        out.append(np.kron(real_form(cos[par::2, :half], sin[par::2, :half]), eye))
    for par in (0, 1):
        out.append(np.kron(real_form(cos[par::2, :half].T, -sin[par::2, :half].T), eye))
    return rounded(np.stack(out))


def dot(a, b):
    return jnp.dot(a, b, preferred_element_type=jnp.float32)


def patch_pair_kernel(counts_ref, obs_ref, mask_ref, table_ref, out_ref, mid, mid2, held, free, top):
    extent = obs_ref.shape[1]
    plane = obs_ref.shape[2]
    half = extent // 2
    lanes = obs_ref.shape[3]
    freq = lanes // 2
    hp = plane // 2
    first = pl.program_id(0) * 2
    count0, count1 = counts_ref[first], counts_ref[first + 1]
    most = jnp.maximum(count0, count1)
    low_lane = lax.broadcasted_iota(jnp.int32, (plane, lanes), 1) < freq

    def to_mid(m, xe, xo):
        for par, x in ((0, xe), (1, xo)):
            y = dot(table_ref[par], x.astype(jnp.bfloat16))
            lo, hi = y[:, :lanes], y[:, lanes:]
            for sd, v in ((0, lo + hi), (1, lo - hi)):
                v = v.astype(jnp.bfloat16).reshape(2, half, extent, lanes)
                for c in (0, 1):
                    mid[:, sd, c, m, :, par * lanes : (par + 1) * lanes] = v[c]

    def halves(x):
        a, b, c, d = x[:hp], x[hp:plane], x[plane : plane + hp], x[plane + hp :]
        return jnp.concatenate([a + b, c + d], 0), jnp.concatenate([a - b, c - d], 0)

    def begin(m, carry):
        row = lax.broadcasted_iota(jnp.int32, (2 * extent, 2 * lanes), 0)
        lane = lax.broadcasted_iota(jnp.int32, (2 * extent, 2 * lanes), 1)
        wanted = m + jnp.where(lane >= lanes, half, 0) + jnp.where(lane % lanes >= freq, extent, 0)
        pick = jnp.where(row == wanted, 1.0, 0.0).astype(jnp.bfloat16)
        marks = mask_ref[...].reshape(2 * extent, plane)
        spread = lax.dot_general(marks, pick, (((0,), (0,)), ((), ())), preferred_element_type=jnp.float32)
        free[m] = 1.0 - spread
        parts = []
        for hi in (0, 1):
            p0 = obs_ref[0, m + hi * half].astype(jnp.float32)
            p1 = obs_ref[1, m + hi * half].astype(jnp.float32)
            re = jnp.where(low_lane, p0, pltpu.roll(p1, freq, 1))
            im = jnp.where(low_lane, pltpu.roll(p0, freq, 1), p1)
            s = spread[:, hi * lanes : (hi + 1) * lanes]
            parts.append(jnp.concatenate([jnp.where(s > 0, re, 0.0), jnp.where(s > 0, im, 0.0)], 0))
        x = jnp.concatenate(parts, 1)
        held[m] = x.astype(jnp.bfloat16)
        xe, xo = halves(x)
        to_mid(m, xe, xo)
        return carry

    lax.fori_loop(0, half, begin, 0)

    def coefs(k1, sd):
        return dot(table_ref[4 + sd], mid[k1, sd].reshape(plane, 2 * lanes))

    def peak(k1, best):
        for sd in (0, 1):
            c = coefs(k1, sd)
            size = c[:hp] * c[:hp] + c[hp:] * c[hp:]
            best = jnp.maximum(best, jnp.max(size.reshape(hp // 8, 8, 2 * lanes), axis=0))
        return best

    best = lax.fori_loop(0, half, peak, jnp.zeros((8, 2 * lanes), jnp.float32))
    best = jnp.max(best, axis=0, keepdims=True)
    best = jnp.sqrt(jnp.maximum(best[:, :lanes], best[:, lanes:]))
    top[...] = jnp.broadcast_to(jnp.concatenate([best, best], 1) * 0.5, top.shape)

    def shrink(k1, cutoff):
        back = []
        for sd in (0, 1):
            c = coefs(k1, sd)
            re, im = c[:hp], c[hp:]
            square = jnp.maximum(re * re + im * im, 1e-30)
            size = square * lax.rsqrt(square)
            factor = jnp.maximum(size - cutoff, 0.0) * pl.reciprocal(size + 1e-6, approx=True)
            thin = jnp.concatenate([(re * factor).astype(jnp.bfloat16), (im * factor).astype(jnp.bfloat16)], 0)
            back.append(dot(table_ref[6 + sd], thin))
        for ab, v in ((0, back[0] + back[1]), (1, back[0] - back[1])):
            v = v.astype(jnp.bfloat16).reshape(2, half, extent, 2 * lanes)
            for par in (0, 1):
                for c in (0, 1):
                    mid2[:, par, c, k1, :, ab * lanes : (ab + 1) * lanes] = v[c, :, :, par * lanes : (par + 1) * lanes]
        return cutoff

    def returned(m):
        e = dot(table_ref[2], mid2[m, 0].reshape(plane, 2 * lanes))
        o = dot(table_ref[3], mid2[m, 1].reshape(plane, 2 * lanes))
        s, d = e + o, e - o
        open_ = free[m]
        obs = held[m].astype(jnp.float32)
        re = obs[:plane] + open_ * jnp.concatenate([s[:hp], d[:hp]], 0)
        im = obs[plane:] + open_ * jnp.concatenate([s[hp:], d[hp:]], 0)
        return re, im

    def again(m, carry):
        re, im = returned(m)
        xe, xo = halves(jnp.concatenate([re, im], 0))
        to_mid(m, xe, xo)
        return carry

    def sweep(k, carry):
        cutoff = top[0:1]
        lax.fori_loop(0, half, shrink, cutoff)
        top[...] = top[...] * 0.6
        ends0, ends1 = k == count0 - 1, k == count1 - 1

        def give(m, carry):
            re, im = returned(m)
            for hi in (0, 1):
                r, i = re[:, hi * lanes : (hi + 1) * lanes], im[:, hi * lanes : (hi + 1) * lanes]

                @pl.when(ends0)
                def _():
                    out_ref[0, m + hi * half] = jnp.where(low_lane, r, pltpu.roll(i, freq, 1)).astype(jnp.bfloat16)

                @pl.when(ends1)
                def _():
                    out_ref[1, m + hi * half] = jnp.where(low_lane, pltpu.roll(r, freq, 1), i).astype(jnp.bfloat16)

            @pl.when(k < most - 1)
            def _():
                xe, xo = halves(jnp.concatenate([re, im], 0))
                to_mid(m, xe, xo)

            return carry

        @pl.when(ends0 | ends1)
        def _():
            lax.fori_loop(0, half, give, 0)

        @pl.when(jnp.logical_not(ends0 | ends1))
        def _():
            lax.fori_loop(0, half, again, 0)

        return carry

    lax.fori_loop(0, most, sweep, 0)


def project(observed, masks, sweeps):
    owned, extent, plane, lanes = observed.shape
    half = extent // 2
    tables = jnp.asarray(dft_blocks(extent))
    block = (2, extent, plane, lanes)
    return pl.pallas_call(
        patch_pair_kernel,
        grid=(owned // 2,),
        out_shape=jax.ShapeDtypeStruct(observed.shape, jnp.bfloat16),
        in_specs=[
            pl.BlockSpec(memory_space=pltpu.SMEM),
            pl.BlockSpec(block, lambda i: (i, 0, 0, 0)),
            pl.BlockSpec((2, extent, plane), lambda i: (i, 0, 0)),
            pl.BlockSpec(tables.shape, lambda i: (0, 0, 0)),
        ],
        out_specs=pl.BlockSpec(block, lambda i: (i, 0, 0, 0)),
        scratch_shapes=[
            pltpu.VMEM((half, 2, 2, half, extent, 2 * lanes), jnp.bfloat16),
            pltpu.VMEM((half, 2, 2, half, extent, 2 * lanes), jnp.bfloat16),
            pltpu.VMEM((half, 2 * plane, 2 * lanes), jnp.bfloat16),
            pltpu.VMEM((half, plane, 2 * lanes), jnp.float32),
            pltpu.VMEM((8, 2 * lanes), jnp.float32),
        ],
        compiler_params=pltpu.CompilerParams(vmem_limit_bytes=48 * 2**20),
        cost_estimate=pl.CostEstimate(flops=owned * 5 * 2**30, bytes_accessed=2**23, transcendentals=2**20),
    )(sweeps, observed, masks.astype(jnp.bfloat16), tables)


def passed_along(block, axis, distance):
    devices = range(lax.axis_size(axis))
    route = [(i - distance, i) for i in devices if i - distance in devices]
    return lax.ppermute(block, axis, route)


def shards(spectra, sampled_mask, counts):
    regrouped = lax.all_to_all(spectra, "shot", split_axis=1, concat_axis=2, tiled=True)
    owned = regrouped.shape[1]
    extent = sampled_mask.shape[2]
    plane = extent * extent
    lanes = regrouped.shape[3]
    observed = regrouped.reshape(owned, extent, plane, lanes)
    result = project(observed, sampled_mask[0], counts[0])
    half = extent // 2
    arrived = passed_along(result[-1, half:], "shot", 1)
    earlier = jnp.concatenate([arrived[None], result[:-1, half:]], axis=0).astype(jnp.float32)
    weight = ((jnp.arange(half, dtype=jnp.float32) + 0.5) / half)[:, None, None]
    mixed = weight * result[:, :half].astype(jnp.float32) + (1.0 - weight) * earlier
    mixed = mixed.astype(jnp.bfloat16).reshape(1, owned, half * plane, lanes)
    return lax.all_to_all(mixed, "shot", split_axis=2, concat_axis=1, tiled=True)


def solution(mesh):
    return jax.shard_map(
        shards,
        mesh=mesh,
        in_specs=(P("az", None, "shot", None), P("az", "shot", None, None), P("az", "shot")),
        out_specs=P("az", None, "shot", None),
        check_vma=False,
    )
```

time: 649 us -> 281 us (0.43)
  matrix products: 198 us -> 0 us
  local copies, waits for them, and re-layouts: 161 us -> 16.5 us
  other arithmetic: 125 us -> 1.06 us
  Pallas kernels: 0 us -> 109 us
  loops' own time: 22.6 us -> 0 us
  blocking collectives: 30.7 us -> 46.3 us
    dot_general x208 -> x0, matrix products: 198 us -> none  [the longest x104 104 us: apply_along(): jnp.einsum(pattern, mat_imag, rotated, preferred_element_type=jnp.float32)]
    pallas_call x0 -> x1, Pallas kernels: none -> 109 us  [project(): pl.pallas_call(patch_pair_kernel, grid=(owned // 2,), out_shape=jax.Shape...]
    convert_element_type x44 -> x0, local copies, waits for them, and re-layouts: 58.7 us -> none  [the longest x28 33.1 us: forward(): apply_along(kron_real, kron_imag, volume, 'kj,ajl->akl')]
    concatenate x28 -> x0, local copies, waits for them, and re-layouts: 33.6 us -> none  [apply_along(): jnp.concatenate([-volume[..., halfway:], volume[..., :halfway]], axis=-1)]
    while x144 -> x0, local copies, waits for them, and re-layouts: 33.5 us -> none
    div x25 -> x1, other arithmetic: 28.9 us -> 0.01 us  [shards(): weight = ((jnp.arange(half, dtype=jnp.float32) + 0.5) / half)[:, None, None]]
    neg x112 -> x0, other arithmetic: 25.1 us -> none  [the longest x104 24.8 us: apply_along(): -volume[..., halfway:]]
    another operation x5 -> x0, loops' own time: 22.6 us -> none  [the longest x4 21.9 us: project_patch(): return lax.fori_loop(0, sweeps, sweep_step, initial)]
where the time goes in v1:
time: 281 us
  Pallas kernels  109 us (39%)
  waiting for transfers between devices  99.7 us (35%)
  blocking collectives  46.3 us (16%)
  local copies, waits for them, and re-layouts  16.5 us (6%)
  starting transfers between devices  8.71 us (3%)
    pallas_call x1, Pallas kernels, project(): pl.pallas_call(patch_pair_kernel, grid=(owned // 2,), out_shape=jax.Shape...  109 us
    all_to_all x1, waiting for transfers between devices, shards(): lax.all_to_all(spectra, 'shot', split_axis=1, concat_axis=2, tiled=True)  93.3 us
    all_to_all x1, blocking collectives, shards(): lax.all_to_all(mixed, 'shot', split_axis=2, concat_axis=1, tiled=True)  46.3 us
    reshape x1, local copies, waits for them, and re-layouts, shards(): mixed = mixed.astype(jnp.bfloat16).reshape(1, owned, half * plane, lanes)  9.76 us
    all_to_all x1, starting transfers between devices, shards(): lax.all_to_all(spectra, 'shot', split_axis=1, concat_axis=2, tiled=True)  7.38 us
    ppermute x1, waiting for transfers between devices, passed_along(): return lax.ppermute(block, axis, route)  6.48 us
  transfers between devices with their start and end apart: 2, of which 2 were waited for; matrix products, arithmetic and copies ran while one was open for 0% of the time, Pallas kernels for 0%

profile of v1, /device:TPU:0, one launch (start us, length us, event | category | flops | bytes accessed | tf_op | source)
XLA Modules:
  0.0 281.3 jit_solution(3810962648004754060)
XLA Ops:
  0.0 0.0 copy-start.2
  0.0 7.4 %all-to-all-start = ((bf16[1,32,512,128]{3,2,0,1:T(8,128)(2,1)}), bf16[1,32,512,128]{3,2,0,1:T(8,128)(2,1)}, u32[]{:S(2)}, u32[]{:S(2)}) async-start(bf16[1,32,512,128]{3,2,0,1:T(8,128)(2,1)} %bitcast.19), calls=%async_computation | async-start | bytes 8388608 | tf_op jit(solution)/shard_map/all_to_all | solution.py:220
  7.4 0.0 copy-done.2
  7.4 93.3 %all-to-all-done = bf16[1,32,512,128]{3,2,0,1:T(8,128)(2,1)} async-done(((bf16[1,32,512,128]{3,2,0,1:T(8,128)(2,1)}), bf16[1,32,512,128]{3,2,0,1:T(8,128)(2,1)}, u32[]{:S(2)}, u32[]{:S(2)}) %all-to-all-start) | async-done | bytes 4194336 | tf_op jit(solution)/shard_map/all_to_all | solution.py:220
  100.7 0.0 copy-start
  100.7 0.0 copy-start.1
  100.7 4.7 %copy.8 = bf16[1,8,4,512,128]{4,3,1,2,0:T(8,128)(2,1)} copy(bf16[1,8,4,512,128]{4,3,2,1,0:T(8,128)(2,1)} %bitcast.2) | data formatting | bytes 8388608 | tf_op jit(solution)/shard_map/all_to_all | solution.py:220
  105.4 0.0 copy-done
  105.4 0.0 copy-done.1
  105.4 108.9 %shard_map.46 = bf16[4,16,256,128]{3,2,1,0:T(8,128)(2,1)S(1)} custom-call(s32[4]{0:T(128)S(1)} %bitcast.16, bf16[4,16,256,128]{3,2,1,0:T(8,128)(2,1)} %bitcast.20, bf16[4,16,256]{2,1,0:T(8,128)(2,1)S(1)} %convert_bitcast_fusion.mask_ref, bf16[8,256,256]{2,1,0:T(8,128)(2,1)S(1)} %copy-done.1), custom_call_target="tpu_custom_call" | custom-call | flops 21474836480 | bytes 8388608 | tf_op jit(solution)/shard_map/pallas_call | solution.py:190
  214.3 1.3 collective-permute-start
  215.7 0.1 slice.14
  215.8 6.5 %collective-permute-done = bf16[8,256,128]{2,1,0:T(8,128)(2,1)S(1)} collective-permute-done((bf16[8,256,128]{2,1,0:T(8,128)(2,1)S(1)}, bf16[8,256,128]{2,1,0:T(8,128)(2,1)S(1)}, u32[]{:S(2)}, u32[]{:S(2)}) %collective-permute-start) | collective-permute-done | bytes 524320 | tf_op jit(solution)/shard_map/ppermute | solution.py:216
  222.3 1.0 add_convert_fusion
  223.3 9.8 %copy.9 = bf16[1,4,2048,128]{3,1,0,2:T(4,128)(2,1)S(1)} copy(bf16[1,4,2048,128]{3,2,1,0:T(8,128)(2,1)S(1)} %bitcast.17) | data formatting | bytes 4194304 | tf_op jit(solution)/shard_map/reshape | solution.py:232
  233.1 46.3 %all_to_all.33 = bf16[1,4,2048,128]{3,1,0,2:T(4,128)(2,1)S(1)} all-to-all(bf16[1,4,2048,128]{3,1,0,2:T(4,128)(2,1)S(1)} %copy.9), channel_id=1, replica_groups=mesh['shot'=8,'az'=4] {'shot'}, dimensions={2} | all-to-all | bytes 4194304 | tf_op jit(solution)/shard_map/all_to_all | solution.py:233
  279.4 1.8 copy.10
  (3 shorter events, 0.1 us)
Async XLA Ops:
  0.0 7.4 %copy-start.2 = (s32[1,4,16,256]{3,2,1,0:T(8,128)S(1)}, s32[1,4,16,256]{3,2,1,0:T(8,128)}, u32[]{:S(2)}) copy-start(s32[1,4,16,256]{3,2,1,0:T(8,128)} %param.5) | copy-start | bytes 196612
  0.0 100.7 %all-to-all-start = ((bf16[1,32,512,128]{3,2,0,1:T(8,128)(2,1)}), bf16[1,32,512,128]{3,2,0,1:T(8,128)(2,1)}, u32[]{:S(2)}, u32[]{:S(2)}) async-start(bf16[1,32,512,128]{3,2,0,1:T(8,128)(2,1)} %bitcast.19), calls=%async_computation | async-start | bytes 8388608 | tf_op jit(solution)/shard_map/all_to_all | solution.py:220
  100.7 4.7 %copy-start = (s32[1,4]{1,0:T(1,128)S(1)}, s32[1,4]{1,0:T(1,128)}, u32[]{:S(2)}) copy-start(s32[1,4]{1,0:T(1,128)} %param.6) | copy-start | bytes 52
  100.7 4.7 %copy-start.1 = (bf16[8,256,256]{2,1,0:T(8,128)(2,1)S(1)}, bf16[8,256,256]{2,1,0:T(8,128)(2,1)}, u32[]{:S(2)}) copy-start(bf16[8,256,256]{2,1,0:T(8,128)(2,1)} %constant.9.clone.table_ref) | copy-start | bytes 3145732
  214.3 8.0 %collective-permute-start = (bf16[8,256,128]{2,1,0:T(8,128)(2,1)S(1)}, bf16[8,256,128]{2,1,0:T(8,128)(2,1)S(1)}, u32[]{:S(2)}, u32[]{:S(2)}) collective-permute-start(bf16[8,256,128]{2,1,0:T(8,128)(2,1)S(1)} %slice_bitcast_fusion), channel_id=1, source_target_pairs={{0,4},{4,8},{8,12},{12,16},{16,20},{20,24},{24,28},{1,5},{5,9},{9,... | collective-permute-start | bytes 1572872 | tf_op jit(solution)/shard_map/ppermute | solution.py:216

commit v2 on v1

--- a/solution.py
+++ b/solution.py
@@ -47,16 +47,24 @@
 
 
 def patch_pair_kernel(counts_ref, obs_ref, mask_ref, table_ref, out_ref, mid, mid2, held, free, top):
-    extent = obs_ref.shape[1]
-    plane = obs_ref.shape[2]
+    extent, plane = mask_ref.shape[1:]
+    rows = obs_ref.shape[2]
     half = extent // 2
     lanes = obs_ref.shape[3]
     freq = lanes // 2
     hp = plane // 2
-    first = pl.program_id(0) * 2
-    count0, count1 = counts_ref[first], counts_ref[first + 1]
+    count0, count1 = counts_ref[0], counts_ref[1]
     most = jnp.maximum(count0, count1)
     low_lane = lax.broadcasted_iota(jnp.int32, (plane, lanes), 1) < freq
+
+    def observed(p, a):
+        if rows >= plane:
+            per = rows // plane
+            block = obs_ref[a // per, p, pl.ds(pl.multiple_of(a % per * plane, plane), plane)]
+        else:
+            per = plane // rows
+            block = obs_ref[pl.ds(a * per, per), p].reshape(plane, lanes)
+        return block.astype(jnp.float32)
 
     def to_mid(m, xe, xo):
         for par, x in ((0, xe), (1, xo)):
@@ -81,8 +89,8 @@
         free[m] = 1.0 - spread
         parts = []
         for hi in (0, 1):
-            p0 = obs_ref[0, m + hi * half].astype(jnp.float32)
-            p1 = obs_ref[1, m + hi * half].astype(jnp.float32)
+            p0 = observed(0, m + hi * half)
+            p1 = observed(1, m + hi * half)
             re = jnp.where(low_lane, p0, pltpu.roll(p1, freq, 1))
             im = jnp.where(low_lane, pltpu.roll(p0, freq, 1), p1)
             s = spread[:, hi * lanes : (hi + 1) * lanes]
@@ -93,7 +101,7 @@
         to_mid(m, xe, xo)
         return carry
 
-    lax.fori_loop(0, half, begin, 0)
+    lax.fori_loop(0, half, begin, 0, unroll=8)
 
     def coefs(k1, sd):
         return dot(table_ref[4 + sd], mid[k1, sd].reshape(plane, 2 * lanes))
@@ -105,7 +113,7 @@
             best = jnp.maximum(best, jnp.max(size.reshape(hp // 8, 8, 2 * lanes), axis=0))
         return best
 
-    best = lax.fori_loop(0, half, peak, jnp.zeros((8, 2 * lanes), jnp.float32))
+    best = lax.fori_loop(0, half, peak, jnp.zeros((8, 2 * lanes), jnp.float32), unroll=8)
     best = jnp.max(best, axis=0, keepdims=True)
     best = jnp.sqrt(jnp.maximum(best[:, :lanes], best[:, lanes:]))
     top[...] = jnp.broadcast_to(jnp.concatenate([best, best], 1) * 0.5, top.shape)
@@ -145,7 +153,7 @@
 
     def sweep(k, carry):
         cutoff = top[0:1]
-        lax.fori_loop(0, half, shrink, cutoff)
+        lax.fori_loop(0, half, shrink, cutoff, unroll=8)
         top[...] = top[...] * 0.6
         ends0, ends1 = k == count0 - 1, k == count1 - 1
 
@@ -171,33 +179,27 @@
 
         @pl.when(ends0 | ends1)
         def _():
-            lax.fori_loop(0, half, give, 0)
+            lax.fori_loop(0, half, give, 0, unroll=8)
 
         @pl.when(jnp.logical_not(ends0 | ends1))
         def _():
-            lax.fori_loop(0, half, again, 0)
+            lax.fori_loop(0, half, again, 0, unroll=8)
 
         return carry
 
     lax.fori_loop(0, most, sweep, 0)
 
 
-def project(observed, masks, sweeps):
-    owned, extent, plane, lanes = observed.shape
+def project(received, masks, sweeps, tables):
+    lanes = received.shape[3]
+    extent, plane = masks.shape[1:]
     half = extent // 2
-    tables = jnp.asarray(dft_blocks(extent))
-    block = (2, extent, plane, lanes)
+    whole = pl.BlockSpec(memory_space=pltpu.VMEM)
     return pl.pallas_call(
         patch_pair_kernel,
-        grid=(owned // 2,),
-        out_shape=jax.ShapeDtypeStruct(observed.shape, jnp.bfloat16),
-        in_specs=[
-            pl.BlockSpec(memory_space=pltpu.SMEM),
-            pl.BlockSpec(block, lambda i: (i, 0, 0, 0)),
-            pl.BlockSpec((2, extent, plane), lambda i: (i, 0, 0)),
-            pl.BlockSpec(tables.shape, lambda i: (0, 0, 0)),
-        ],
-        out_specs=pl.BlockSpec(block, lambda i: (i, 0, 0, 0)),
+        out_shape=jax.ShapeDtypeStruct((2, extent, plane, lanes), jnp.bfloat16),
+        in_specs=[pl.BlockSpec(memory_space=pltpu.SMEM), whole, whole, whole],
+        out_specs=whole,
         scratch_shapes=[
             pltpu.VMEM((half, 2, 2, half, extent, 2 * lanes), jnp.bfloat16),
             pltpu.VMEM((half, 2, 2, half, extent, 2 * lanes), jnp.bfloat16),
@@ -205,9 +207,9 @@
             pltpu.VMEM((half, plane, 2 * lanes), jnp.float32),
             pltpu.VMEM((8, 2 * lanes), jnp.float32),
         ],
-        compiler_params=pltpu.CompilerParams(vmem_limit_bytes=48 * 2**20),
-        cost_estimate=pl.CostEstimate(flops=owned * 5 * 2**30, bytes_accessed=2**23, transcendentals=2**20),
-    )(sweeps, observed, masks.astype(jnp.bfloat16), tables)
+        compiler_params=pltpu.CompilerParams(vmem_limit_bytes=40 * 2**20),
+        cost_estimate=pl.CostEstimate(flops=40 * 2**30, bytes_accessed=2**23, transcendentals=2**20),
+    )(sweeps, received, masks.astype(jnp.bfloat16), tables)
 
 
 def passed_along(block, axis, distance):
@@ -216,21 +218,37 @@
     return lax.ppermute(block, axis, route)
 
 
+def exchanged(parts):
+    return lax.all_to_all(parts, "shot", split_axis=0, concat_axis=0, tiled=True)
+
+
 def shards(spectra, sampled_mask, counts):
-    regrouped = lax.all_to_all(spectra, "shot", split_axis=1, concat_axis=2, tiled=True)
-    owned = regrouped.shape[1]
-    extent = sampled_mask.shape[2]
-    plane = extent * extent
-    lanes = regrouped.shape[3]
-    observed = regrouped.reshape(owned, extent, plane, lanes)
-    result = project(observed, sampled_mask[0], counts[0])
+    devices = lax.axis_size("shot")
+    owned, extent, plane = sampled_mask.shape[1:]
+    rows, lanes = spectra.shape[2:]
     half = extent // 2
-    arrived = passed_along(result[-1, half:], "shot", 1)
-    earlier = jnp.concatenate([arrived[None], result[:-1, half:]], axis=0).astype(jnp.float32)
+    tables = jnp.asarray(dft_blocks(extent))
+    by_owner = spectra.reshape(devices, owned, rows, lanes)
+    starts = range(owned - 2, -1, -2)
+    received = [exchanged(by_owner[:, s : s + 2]) for s in starts]
     weight = ((jnp.arange(half, dtype=jnp.float32) + 0.5) / half)[:, None, None]
-    mixed = weight * result[:, :half].astype(jnp.float32) + (1.0 - weight) * earlier
-    mixed = mixed.astype(jnp.bfloat16).reshape(1, owned, half * plane, lanes)
-    return lax.all_to_all(mixed, "shot", split_axis=2, concat_axis=1, tiled=True)
+
+    def blend(own, earlier):
+        mixed = weight * own.astype(jnp.float32) + (1.0 - weight) * earlier.astype(jnp.float32)
+        return mixed.astype(jnp.bfloat16).reshape(devices, half * plane // devices, lanes)
+
+    lower = None
+    for part, s in zip(received, starts):
+        result = project(part, sampled_mask[0, s : s + 2], counts[0, s : s + 2], tables)
+        if lower is None:
+            arrived = passed_along(result[1, half:], "shot", 1)
+            last = exchanged(blend(result[1, :half], result[0, half:]))[:, None]
+            late = []
+        else:
+            late = [blend(result[1, :half], result[0, half:]), blend(lower, result[1, half:])] + late
+        lower = result[0, :half]
+    late = [blend(lower, arrived)] + late
+    return jnp.concatenate([exchanged(jnp.stack(late, 1)), last], 1).reshape(1, devices * owned, half * plane // devices, lanes)
 
 
 def solution(mesh):

time: 281 us -> 213 us (0.76)
  Pallas kernels: 109 us -> 66.5 us
  waiting for transfers between devices: 99.7 us -> 71.3 us
  starting transfers between devices: 8.71 us -> 19.2 us
  blocking collectives: 46.3 us -> 39.7 us
  local copies, waits for them, and re-layouts: 16.5 us -> 9.98 us
  other arithmetic: 1.06 us -> 5.85 us
    pallas_call x1 -> x2, Pallas kernels: 109 us -> 66.5 us  [project(): pl.pallas_call(patch_pair_kernel, out_shape=jax.ShapeDtypeStruct((2, exte...]
    all_to_all x1 -> x3, waiting for transfers between devices: 93.3 us -> 71.3 us  [exchanged(): lax.all_to_all(parts, 'shot', split_axis=0, concat_axis=0, tiled=True)]
    reshape x1 -> x0, local copies, waits for them, and re-layouts: 9.76 us -> none  [shards(): mixed = mixed.astype(jnp.bfloat16).reshape(1, owned, half * plane, lanes)]
    all_to_all x1 -> x3, starting transfers between devices: 7.38 us -> 17.1 us  [exchanged(): lax.all_to_all(parts, 'shot', split_axis=0, concat_axis=0, tiled=True)]
    all_to_all x1, blocking collectives: 46.3 us -> 39.7 us  [exchanged(): lax.all_to_all(parts, 'shot', split_axis=0, concat_axis=0, tiled=True)]
    all_to_all x2 -> x0, local copies, waits for them, and re-layouts: 6.55 us -> none  [the longest x1 4.7 us: shards(): lax.all_to_all(spectra, 'shot', split_axis=1, concat_axis=2, tiled=True)]
    ppermute x1, waiting for transfers between devices: 6.48 us -> 0.01 us  [passed_along(): return lax.ppermute(block, axis, route)]
    slice x1, local copies, waits for them, and re-layouts: 0.15 us -> 4.7 us  [shards(): received = [exchanged(by_owner[:, s:s + 2]) for s in starts]]
  transfers between devices with their start and end apart: 2 -> 4, of which waited for: 2 -> 3; matrix products, arithmetic and copies ran while one was open for 0% -> 1% of each run, Pallas kernels for 0% -> 31%
where the time goes in v2:
time: 213 us
  waiting for transfers between devices  71.3 us (33%)
  Pallas kernels  66.5 us (31%)
  blocking collectives  39.7 us (19%)
  starting transfers between devices  19.2 us (9%)
  local copies, waits for them, and re-layouts  9.98 us (5%)
  other arithmetic  5.85 us (3%)
    all_to_all x3, waiting for transfers between devices, exchanged(): lax.all_to_all(parts, 'shot', split_axis=0, concat_axis=0, tiled=True)  71.3 us
    pallas_call x2, Pallas kernels, project(): pl.pallas_call(patch_pair_kernel, out_shape=jax.ShapeDtypeStruct((2, exte...  66.5 us
    all_to_all x1, blocking collectives, exchanged(): lax.all_to_all(parts, 'shot', split_axis=0, concat_axis=0, tiled=True)  39.7 us
    all_to_all x3, starting transfers between devices, exchanged(): lax.all_to_all(parts, 'shot', split_axis=0, concat_axis=0, tiled=True)  17.1 us
    slice x1, local copies, waits for them, and re-layouts, shards(): received = [exchanged(by_owner[:, s:s + 2]) for s in starts]  4.7 us
  transfers between devices with their start and end apart: 4, of which 3 were waited for; matrix products, arithmetic and copies ran while one was open for 1% of the time, Pallas kernels for 31%

profile of v2, /device:TPU:0, one launch (start us, length us, event | category | flops | bytes accessed | tf_op | source)
XLA Modules:
  0.0 212.6 jit_solution(6810529351802863567)
XLA Ops:
  0.0 4.7 %fusion.9 = (bf16[8,2,512,128]{3,2,1,0:T(8,128)(2,1)}, bf16[8,2,512,128]{3,2,1,0:T(8,128)(2,1)}) fusion(bf16[8,4,512,128]{3,2,1,0:T(8,128)(2,1)} %bitcast.52), kind=kLoop, calls=%fused_computation.32 | loop fusion | bytes 8388608 | tf_op jit(solution)/shard_map/slice | solution.py:233
  4.7 0.0 copy-start.4
  4.7 0.0 copy-start.5
  4.7 7.4 %all-to-all-start.1 = ((bf16[8,2,512,128]{3,2,1,0:T(8,128)(2,1)}), bf16[8,2,512,128]{3,2,1,0:T(8,128)(2,1)S(1)}, u32[]{:S(2)}, u32[]{:S(2)}) async-start(bf16[8,2,512,128]{3,2,1,0:T(8,128)(2,1)} %get-tuple-element.6), calls=%async_computation.1 | async-start | bytes 4194304 | tf_op jit(solution)/shard_map/all_to_all | solution.py:222
  12.1 0.0 copy-done.4
  12.1 0.0 copy-done.5
  12.1 0.1 slice_bitcast_fusion.11
  12.2 48.1 %all-to-all-done.1.obs_ref = bf16[8,2,512,128]{3,2,1,0:T(8,128)(2,1)S(1)} async-done(((bf16[8,2,512,128]{3,2,1,0:T(8,128)(2,1)}), bf16[8,2,512,128]{3,2,1,0:T(8,128)(2,1)S(1)}, u32[]{:S(2)}, u32[]{:S(2)}) %all-to-all-start.1) | async-done | bytes 2097184 | tf_op jit(solution)/shard_map/all_to_all | solution.py:222
  60.3 0.0 copy-start
  60.3 0.0 copy-start.3
  60.3 1.3 copy-done
  61.7 4.4 %all-to-all-start = ((bf16[8,2,512,128]{3,2,1,0:T(8,128)(2,1)}), bf16[8,2,512,128]{3,2,1,0:T(8,128)(2,1)}, u32[]{:S(2)}, u32[]{:S(2)}) async-start(bf16[8,2,512,128]{3,2,1,0:T(8,128)(2,1)} %get-tuple-element.5), calls=%async_computation | async-start | bytes 4194304 | tf_op jit(solution)/shard_map/all_to_all | solution.py:222
  66.0 0.0 copy-done.3
  66.0 0.0 copy-start.1
  66.0 1.6 copy-done.1
  67.6 32.7 %shard_map.47 = bf16[2,16,256,128]{3,2,1,0:T(8,128)(2,1)S(1)} custom-call(s32[2]{0:T(128)S(1)} %get-tuple-element.14.counts_ref, bf16[8,2,512,128]{3,2,1,0:T(8,128)(2,1)S(1)} %copy-done.1, bf16[2,16,256]{2,1,0:T(8,128)(2,1)S(1)} %get-tuple-element.10.mask_ref, bf16[8,256,256]{2,1,0:T(8,128)(2,1)S(1)} %copy-done.3), custom_call_target="tpu_custom_call" | custom-call | flops 42949672960 | bytes 8388608 | tf_op jit(solution)/shard_map/pallas_call | solution.py:198
  100.3 0.8 slice_bitcast_fusion.6
  101.2 2.1 collective-permute-start
  103.3 10.6 %all-to-all-done.obs_ref = bf16[8,2,512,128]{3,2,1,0:T(8,128)(2,1)} async-done(((bf16[8,2,512,128]{3,2,1,0:T(8,128)(2,1)}), bf16[8,2,512,128]{3,2,1,0:T(8,128)(2,1)}, u32[]{:S(2)}, u32[]{:S(2)}) %all-to-all-start) | async-done | bytes 2097184 | tf_op jit(solution)/shard_map/all_to_all | solution.py:222
  113.9 33.8 %shard_map.46 = bf16[2,16,256,128]{3,2,1,0:T(8,128)(2,1)S(1)} custom-call(s32[2]{0:T(128)S(1)} %get-tuple-element.13.counts_ref, bf16[8,2,512,128]{3,2,1,0:T(8,128)(2,1)} %all-to-all-done.obs_ref, bf16[2,16,256]{2,1,0:T(8,128)(2,1)S(1)} %get-tuple-element.9.mask_ref, bf16[8,256,256]{2,1,0:T(8,128)(2,1)S(1)} %copy-done.3), custom_call_target="tpu_custom_call" | custom-call | flops 42949672960 | bytes 8388608 | tf_op jit(solution)/shard_map/pallas_call | solution.py:198
  147.7 0.0 copy-start.2
  147.7 0.0 collective-permute-done
  147.7 1.3 copy-done.2
  149.0 2.3 %fusion.8 = (bf16[8,1,256,128]{3,2,0,1:T(8,128)(2,1)S(1)}, bf16[8,256,128]{2,1,0:T(8,128)(2,1)}) fusion(bf16[8,256,128]{2,1,0:T(8,128)(2,1)} %collective-permute-done, bf16[2,16,256,128]{3,2,1,0:T(8,128)(2,1)S(1)} %shard_map.46, f32[8]{0:T(128)S(1)} %get-tuple-element.16, f32[8]{0:T(128)S(1)} %get-tuple-element.15, bf16[2,16,256,128]{3,2,1,0:T(8,128)(2,1)S(1)} %shard_map.47), kind=kLoop, calls=%fused_computation.17 | loop fusion | flops 3145728 | bytes 3145792 | tf_op jit(solution)/shard_map/stack | solution.py:251
  151.3 5.3 %all-to-all-start.3 = ((bf16[8,256,128]{2,1,0:T(8,128)(2,1)}), bf16[8,256,128]{2,1,0:T(8,128)(2,1)S(1)}, u32[]{:S(2)}, u32[]{:S(2)}) async-start(bf16[8,256,128]{2,1,0:T(8,128)(2,1)} %get-tuple-element.12), calls=%async_computation.3 | async-start | bytes 1048576 | tf_op jit(solution)/shard_map/all_to_all | solution.py:222
  156.6 1.8 fusion.5
  158.5 0.2 pad_maximum_fusion.1
  158.6 0.1 copy.6
  158.8 12.6 %all-to-all-done.3 = bf16[8,256,128]{2,1,0:T(8,128)(2,1)S(1)} async-done(((bf16[8,256,128]{2,1,0:T(8,128)(2,1)}), bf16[8,256,128]{2,1,0:T(8,128)(2,1)S(1)}, u32[]{:S(2)}, u32[]{:S(2)}) %all-to-all-start.3) | async-done | bytes 524320 | tf_op jit(solution)/shard_map/all_to_all | solution.py:222
  171.4 39.7 %all_to_all.20 = bf16[8,3,256,128]{3,2,1,0:T(8,128)(2,1)S(1)} all-to-all(bf16[8,3,256,128]{3,2,1,0:T(8,128)(2,1)S(1)} %copy.6), channel_id=1, replica_groups=mesh['shot'=8,'az'=4] {'shot'}, dimensions={0} | all-to-all | bytes 3145728 | tf_op jit(solution)/shard_map/all_to_all | solution.py:222
  211.1 1.5 pad_maximum_fusion
  (3 shorter events, 0.0 us)
Async XLA Ops:
  4.7 7.4 %copy-start.4 = (s32[1,4,16,256]{3,2,1,0:T(8,128)S(1)}, s32[1,4,16,256]{3,2,1,0:T(8,128)}, u32[]{:S(2)}) copy-start(s32[1,4,16,256]{3,2,1,0:T(8,128)} %param.5) | copy-start | bytes 196612
  4.7 7.4 %copy-start.5 = (s32[1,4]{1,0:T(1,128)S(1)}, s32[1,4]{1,0:T(1,128)}, u32[]{:S(2)}) copy-start(s32[1,4]{1,0:T(1,128)} %param.6) | copy-start | bytes 52
  4.7 55.6 %all-to-all-start.1 = ((bf16[8,2,512,128]{3,2,1,0:T(8,128)(2,1)}), bf16[8,2,512,128]{3,2,1,0:T(8,128)(2,1)S(1)}, u32[]{:S(2)}, u32[]{:S(2)}) async-start(bf16[8,2,512,128]{3,2,1,0:T(8,128)(2,1)} %get-tuple-element.6), calls=%async_computation.1 | async-start | bytes 4194304 | tf_op jit(solution)/shard_map/all_to_all | solution.py:222
  60.3 1.3 copy-start
  60.3 5.7 %copy-start.3 = (bf16[8,256,256]{2,1,0:T(8,128)(2,1)S(1)}, bf16[8,256,256]{2,1,0:T(8,128)(2,1)}, u32[]{:S(2)}) copy-start(bf16[8,256,256]{2,1,0:T(8,128)(2,1)} %constant.9.clone.table_ref) | copy-start | bytes 3145732
  61.7 52.2 %all-to-all-start = ((bf16[8,2,512,128]{3,2,1,0:T(8,128)(2,1)}), bf16[8,2,512,128]{3,2,1,0:T(8,128)(2,1)}, u32[]{:S(2)}, u32[]{:S(2)}) async-start(bf16[8,2,512,128]{3,2,1,0:T(8,128)(2,1)} %get-tuple-element.5), calls=%async_computation | async-start | bytes 4194304 | tf_op jit(solution)/shard_map/all_to_all | solution.py:222
  66.0 1.6 copy-start.1
  101.2 46.5 %collective-permute-start = (bf16[8,256,128]{2,1,0:T(8,128)(2,1)}, bf16[8,256,128]{2,1,0:T(8,128)(2,1)}, u32[]{:S(2)}, u32[]{:S(2)}) collective-permute-start(bf16[8,256,128]{2,1,0:T(8,128)(2,1)} %slice_bitcast_fusion.6), channel_id=1, source_target_pairs={{0,4},{4,8},{8,12},{12,16},{16,20},{20,24},{24,28},{1,5},{5,9},{9,... | collective-permute-start | bytes 1572872 | tf_op jit(solution)/shard_map/ppermute | solution.py:218
  147.7 1.3 copy-start.2
  151.3 20.1 %all-to-all-start.3 = ((bf16[8,256,128]{2,1,0:T(8,128)(2,1)}), bf16[8,256,128]{2,1,0:T(8,128)(2,1)S(1)}, u32[]{:S(2)}, u32[]{:S(2)}) async-start(bf16[8,256,128]{2,1,0:T(8,128)(2,1)} %get-tuple-element.12), calls=%async_computation.3 | async-start | bytes 1048576 | tf_op jit(solution)/shard_map/all_to_all | solution.py:222

commit v3 on v2

--- a/solution.py
+++ b/solution.py
@@ -238,11 +238,15 @@
         return mixed.astype(jnp.bfloat16).reshape(devices, half * plane // devices, lanes)
 
     lower = None
-    for part, s in zip(received, starts):
+    for i, s in enumerate(starts):
+        part = received[i]
         result = project(part, sampled_mask[0, s : s + 2], counts[0, s : s + 2], tables)
         if lower is None:
             arrived = passed_along(result[1, half:], "shot", 1)
-            last = exchanged(blend(result[1, :half], result[0, half:]))[:, None]
+            first = blend(result[1, :half], result[0, half:])
+            if len(received) > 1:
+                first, received[1] = lax.optimization_barrier((first, received[1]))
+            last = exchanged(first)[:, None]
             late = []
         else:
             late = [blend(result[1, :half], result[0, half:]), blend(lower, result[1, half:])] + late

time: 213 us -> 202 us (0.948)
  waiting for transfers between devices: 71.3 us -> 59.6 us
    all_to_all x3, waiting for transfers between devices: 71.3 us -> 59.6 us  [exchanged(): lax.all_to_all(parts, 'shot', split_axis=0, concat_axis=0, tiled=True)]
  transfers between devices with their start and end apart: 4 -> 4, of which waited for: 3 -> 2; matrix products, arithmetic and copies ran while one was open for 1% -> 3% of each run, Pallas kernels for 31% -> 32%
where the time goes in v3:
time: 202 us
  Pallas kernels  65.4 us (32%)
  waiting for transfers between devices  59.6 us (30%)
  blocking collectives  41.5 us (21%)
  starting transfers between devices  19.6 us (10%)
  local copies, waits for them, and re-layouts  9.36 us (5%)
  other arithmetic  6.65 us (3%)
    pallas_call x2, Pallas kernels, project(): pl.pallas_call(patch_pair_kernel, out_shape=jax.ShapeDtypeStruct((2, exte...  65.4 us
    all_to_all x3, waiting for transfers between devices, exchanged(): lax.all_to_all(parts, 'shot', split_axis=0, concat_axis=0, tiled=True)  59.6 us
    all_to_all x1, blocking collectives, exchanged(): lax.all_to_all(parts, 'shot', split_axis=0, concat_axis=0, tiled=True)  41.5 us
    all_to_all x3, starting transfers between devices, exchanged(): lax.all_to_all(parts, 'shot', split_axis=0, concat_axis=0, tiled=True)  15.5 us
    slice x1, local copies, waits for them, and re-layouts, shards(): received = [exchanged(by_owner[:, s:s + 2]) for s in starts]  4.71 us
    ppermute x1, starting transfers between devices, passed_along(): return lax.ppermute(block, axis, route)  4.17 us
  transfers between devices with their start and end apart: 4, of which 2 were waited for; matrix products, arithmetic and copies ran while one was open for 3% of the time, Pallas kernels for 32%

profile of v3, /device:TPU:0, one launch (start us, length us, event | category | flops | bytes accessed | tf_op | source)
XLA Modules:
  0.0 202.3 jit_solution(12083092062080256843)
XLA Ops:
  0.0 4.7 %fusion.9 = (bf16[8,2,512,128]{3,2,1,0:T(8,128)(2,1)}, bf16[8,2,512,128]{3,2,1,0:T(8,128)(2,1)}) fusion(bf16[8,4,512,128]{3,2,1,0:T(8,128)(2,1)} %bitcast.52), kind=kLoop, calls=%fused_computation.32 | loop fusion | bytes 8388608 | tf_op jit(solution)/shard_map/slice | solution.py:233
  4.7 0.0 copy-start.4
  4.7 0.0 copy-start.5
  4.7 7.4 %all-to-all-start = ((bf16[8,2,512,128]{3,2,1,0:T(8,128)(2,1)}), bf16[8,2,512,128]{3,2,1,0:T(8,128)(2,1)S(1)}, u32[]{:S(2)}, u32[]{:S(2)}) async-start(bf16[8,2,512,128]{3,2,1,0:T(8,128)(2,1)} %get-tuple-element.10), calls=%async_computation | async-start | bytes 4194304 | tf_op jit(solution)/shard_map/all_to_all | solution.py:222
  12.1 0.0 copy-done.4
  12.1 0.0 copy-done.5
  12.1 0.1 slice_bitcast_fusion.11
  12.2 48.1 %all-to-all-done.obs_ref = bf16[8,2,512,128]{3,2,1,0:T(8,128)(2,1)S(1)} async-done(((bf16[8,2,512,128]{3,2,1,0:T(8,128)(2,1)}), bf16[8,2,512,128]{3,2,1,0:T(8,128)(2,1)S(1)}, u32[]{:S(2)}, u32[]{:S(2)}) %all-to-all-start) | async-done | bytes 2097184 | tf_op jit(solution)/shard_map/all_to_all | solution.py:222
  60.3 0.0 copy-start.1
  60.3 1.3 copy-done.1
  61.7 0.0 copy-start.3
  61.7 3.8 %all-to-all-start.1 = ((bf16[8,2,512,128]{3,2,1,0:T(8,128)(2,1)}), bf16[8,2,512,128]{3,2,1,0:T(8,128)(2,1)S(1)}, u32[]{:S(2)}, u32[]{:S(2)}) async-start(bf16[8,2,512,128]{3,2,1,0:T(8,128)(2,1)} %get-tuple-element.9), calls=%async_computation.1 | async-start | bytes 4194304 | tf_op jit(solution)/shard_map/all_to_all | solution.py:222
  65.5 0.0 copy-done.3
  65.5 0.0 copy-start.2
  65.5 1.6 copy-done.2
  67.1 32.7 %shard_map.46 = bf16[2,16,256,128]{3,2,1,0:T(8,128)(2,1)S(1)} custom-call(s32[2]{0:T(128)S(1)} %get-tuple-element.16.counts_ref, bf16[8,2,512,128]{3,2,1,0:T(8,128)(2,1)S(1)} %copy-done.2, bf16[2,16,256]{2,1,0:T(8,128)(2,1)S(1)} %get-tuple-element.14.mask_ref, bf16[8,256,256]{2,1,0:T(8,128)(2,1)S(1)} %copy-done.3), custom_call_target="tpu_custom_call" | custom-call | flops 42949672960 | bytes 8388608 | tf_op jit(solution)/shard_map/pallas_call | solution.py:198
  99.8 0.0 copy-start
  99.8 0.9 slice_bitcast_fusion.4
  100.7 0.6 copy-done
  101.3 1.1 fusion.7
  102.4 11.5 %all-to-all-done.1.obs_ref = bf16[8,2,512,128]{3,2,1,0:T(8,128)(2,1)S(1)} async-done(((bf16[8,2,512,128]{3,2,1,0:T(8,128)(2,1)}), bf16[8,2,512,128]{3,2,1,0:T(8,128)(2,1)S(1)}, u32[]{:S(2)}, u32[]{:S(2)}) %all-to-all-start.1) | async-done | bytes 2097184 | tf_op jit(solution)/shard_map/all_to_all | solution.py:222
  113.9 4.2 %collective-permute-start = (bf16[8,256,128]{2,1,0:T(8,128)(2,1)}, bf16[8,256,128]{2,1,0:T(8,128)(2,1)}, u32[]{:S(2)}, u32[]{:S(2)}) collective-permute-start(bf16[8,256,128]{2,1,0:T(8,128)(2,1)} %slice_bitcast_fusion.4), channel_id=1, source_target_pairs={{0,4},{4,8},{8,12},{12,16},{16,20},{20,24},{24,28},{1,5},{5,9},{9,... | collective-permute-start | bytes 1572872 | tf_op jit(solution)/shard_map/ppermute | solution.py:218
  118.0 4.3 %all-to-all-start.3 = ((bf16[8,256,128]{2,1,0:T(8,128)(2,1)}), bf16[8,256,128]{2,1,0:T(8,128)(2,1)}, u32[]{:S(2)}, u32[]{:S(2)}) async-start(bf16[8,256,128]{2,1,0:T(8,128)(2,1)} %fusion.7), calls=%async_computation.3 | async-start | bytes 1048576 | tf_op jit(solution)/shard_map/all_to_all | solution.py:222
  122.4 32.7 %shard_map.47 = bf16[2,16,256,128]{3,2,1,0:T(8,128)(2,1)S(1)} custom-call(s32[2]{0:T(128)S(1)} %get-tuple-element.15.counts_ref, bf16[8,2,512,128]{3,2,1,0:T(8,128)(2,1)S(1)} %all-to-all-done.1.obs_ref, bf16[2,16,256]{2,1,0:T(8,128)(2,1)S(1)} %get-tuple-element.13.mask_ref, bf16[8,256,256]{2,1,0:T(8,128)(2,1)S(1)} %copy-done.3), custom_call_target="tpu_custom_call" | custom-call | flops 42949672960 | bytes 8388608 | tf_op jit(solution)/shard_map/pallas_call | solution.py:198
  155.1 1.5 fusion.3
  156.6 0.0 collective-permute-done
  156.6 1.3 fusion.8
  157.9 0.2 pad_maximum_fusion.1
  158.1 0.1 copy.6
  158.3 0.0 all-to-all-done.3
  158.3 41.5 %all_to_all.20 = bf16[8,3,256,128]{3,2,1,0:T(8,128)(2,1)S(1)} all-to-all(bf16[8,3,256,128]{3,2,1,0:T(8,128)(2,1)S(1)} %copy.6), channel_id=1, replica_groups=mesh['shot'=8,'az'=4] {'shot'}, dimensions={0} | all-to-all | bytes 3145728 | tf_op jit(solution)/shard_map/all_to_all | solution.py:222
  199.8 2.5 %pad_maximum_fusion = bf16[8,4,256,128]{3,2,1,0:T(8,128)(2,1)} fusion(bf16[8,1,256,128]{3,2,1,0:T(8,128)(2,1)} %bitcast.15, bf16[8,3,256,128]{3,2,1,0:T(8,128)(2,1)S(1)} %all_to_all.20), kind=kLoop, calls=%fused_computation | loop fusion | flops 1048576 | bytes 4194304 | tf_op jit(solution)/shard_map/concatenate | solution.py:255
  (3 shorter events, 0.0 us)
Async XLA Ops:
  4.7 7.4 %copy-start.4 = (s32[1,4,16,256]{3,2,1,0:T(8,128)S(1)}, s32[1,4,16,256]{3,2,1,0:T(8,128)}, u32[]{:S(2)}) copy-start(s32[1,4,16,256]{3,2,1,0:T(8,128)} %param.5) | copy-start | bytes 196612
  4.7 7.4 %copy-start.5 = (s32[1,4]{1,0:T(1,128)S(1)}, s32[1,4]{1,0:T(1,128)}, u32[]{:S(2)}) copy-start(s32[1,4]{1,0:T(1,128)} %param.6) | copy-start | bytes 52
  4.7 55.6 %all-to-all-start = ((bf16[8,2,512,128]{3,2,1,0:T(8,128)(2,1)}), bf16[8,2,512,128]{3,2,1,0:T(8,128)(2,1)S(1)}, u32[]{:S(2)}, u32[]{:S(2)}) async-start(bf16[8,2,512,128]{3,2,1,0:T(8,128)(2,1)} %get-tuple-element.10), calls=%async_computation | async-start | bytes 4194304 | tf_op jit(solution)/shard_map/all_to_all | solution.py:222
  60.3 1.3 copy-start.1
  61.7 3.8 %copy-start.3 = (bf16[8,256,256]{2,1,0:T(8,128)(2,1)S(1)}, bf16[8,256,256]{2,1,0:T(8,128)(2,1)}, u32[]{:S(2)}) copy-start(bf16[8,256,256]{2,1,0:T(8,128)(2,1)} %constant.9.clone.table_ref) | copy-start | bytes 3145732
  61.7 52.2 %all-to-all-start.1 = ((bf16[8,2,512,128]{3,2,1,0:T(8,128)(2,1)}), bf16[8,2,512,128]{3,2,1,0:T(8,128)(2,1)S(1)}, u32[]{:S(2)}, u32[]{:S(2)}) async-start(bf16[8,2,512,128]{3,2,1,0:T(8,128)(2,1)} %get-tuple-element.9), calls=%async_computation.1 | async-start | bytes 4194304 | tf_op jit(solution)/shard_map/all_to_all | solution.py:222
  65.5 1.6 copy-start.2
  99.8 1.5 copy-start
  113.9 42.7 %collective-permute-start = (bf16[8,256,128]{2,1,0:T(8,128)(2,1)}, bf16[8,256,128]{2,1,0:T(8,128)(2,1)}, u32[]{:S(2)}, u32[]{:S(2)}) collective-permute-start(bf16[8,256,128]{2,1,0:T(8,128)(2,1)} %slice_bitcast_fusion.4), channel_id=1, source_target_pairs={{0,4},{4,8},{8,12},{12,16},{16,20},{20,24},{24,28},{1,5},{5,9},{9,... | collective-permute-start | bytes 1572872 | tf_op jit(solution)/shard_map/ppermute | solution.py:218
  118.0 40.2 %all-to-all-start.3 = ((bf16[8,256,128]{2,1,0:T(8,128)(2,1)}), bf16[8,256,128]{2,1,0:T(8,128)(2,1)}, u32[]{:S(2)}, u32[]{:S(2)}) async-start(bf16[8,256,128]{2,1,0:T(8,128)(2,1)} %fusion.7), calls=%async_computation.3 | async-start | bytes 1048576 | tf_op jit(solution)/shard_map/all_to_all | solution.py:222

commit v4 on v3

--- a/solution.py
+++ b/solution.py
@@ -230,7 +230,10 @@
     tables = jnp.asarray(dft_blocks(extent))
     by_owner = spectra.reshape(devices, owned, rows, lanes)
     starts = range(owned - 2, -1, -2)
-    received = [exchanged(by_owner[:, s : s + 2]) for s in starts]
+    received = []
+    for s in starts:
+        sent, by_owner = lax.optimization_barrier((by_owner[:, s : s + 2], by_owner))
+        received.append(exchanged(sent))
     weight = ((jnp.arange(half, dtype=jnp.float32) + 0.5) / half)[:, None, None]
 
     def blend(own, earlier):

time: 202 us -> 201 us (level); the launches traced: 202 us -> 199 us
  waiting for transfers between devices: 59.6 us -> 56.5 us
    all_to_all x3, waiting for transfers between devices: 59.6 us -> 56.5 us  [exchanged(): lax.all_to_all(parts, 'shot', split_axis=0, concat_axis=0, tiled=True)]
    slice x1 -> x2, local copies, waits for them, and re-layouts: 4.71 us -> 6.24 us  [shards(): sent, by_owner = lax.optimization_barrier((by_owner[:, s:s + 2], by_owner))]
  transfers between devices with their start and end apart: 4 -> 4, of which waited for: 2 -> 2; matrix products, arithmetic and copies ran while one was open for 3% -> 4% of each run, Pallas kernels for 32% -> 33%
where the time goes in v4:
time: 201 us; the launch traced here: 199 us
  Pallas kernels  65.4 us (33%)
  waiting for transfers between devices  56.5 us (28%)
  blocking collectives  39.7 us (20%)
  starting transfers between devices  19.5 us (10%)
  local copies, waits for them, and re-layouts  10.9 us (5%)
  other arithmetic  6.65 us (3%)
    pallas_call x2, Pallas kernels, project(): pl.pallas_call(patch_pair_kernel, out_shape=jax.ShapeDtypeStruct((2, exte...  65.4 us
    all_to_all x3, waiting for transfers between devices, exchanged(): lax.all_to_all(parts, 'shot', split_axis=0, concat_axis=0, tiled=True)  56.5 us
    all_to_all x1, blocking collectives, exchanged(): lax.all_to_all(parts, 'shot', split_axis=0, concat_axis=0, tiled=True)  39.7 us
    all_to_all x3, starting transfers between devices, exchanged(): lax.all_to_all(parts, 'shot', split_axis=0, concat_axis=0, tiled=True)  15.3 us
    slice x2, local copies, waits for them, and re-layouts, shards(): sent, by_owner = lax.optimization_barrier((by_owner[:, s:s + 2], by_owner))  6.24 us
    ppermute x1, starting transfers between devices, passed_along(): return lax.ppermute(block, axis, route)  4.16 us
  transfers between devices with their start and end apart: 4, of which 2 were waited for; matrix products, arithmetic and copies ran while one was open for 4% of the time, Pallas kernels for 33%

profile of v4, /device:TPU:0, one launch (start us, length us, event | category | flops | bytes accessed | tf_op | source)
XLA Modules:
  0.0 198.7 jit_solution(11370612187670501966)
XLA Ops:
  0.0 3.1 %slice.58 = bf16[8,2,512,128]{3,2,1,0:T(8,128)(2,1)} slice(bf16[8,4,512,128]{3,2,1,0:T(8,128)(2,1)} %bitcast.52), slice={[0:8], [2:4], [0:512], [0:128]} | slice | bytes 4194304 | tf_op jit(solution)/shard_map/slice | solution.py:235
  3.1 0.0 copy-start.4
  3.1 7.4 %all-to-all-start = ((bf16[8,2,512,128]{3,2,1,0:T(8,128)(2,1)}), bf16[8,2,512,128]{3,2,1,0:T(8,128)(2,1)S(1)}, u32[]{:S(2)}, u32[]{:S(2)}) async-start(bf16[8,2,512,128]{3,2,1,0:T(8,128)(2,1)} %slice.58), calls=%async_computation | async-start | bytes 4194304 | tf_op jit(solution)/shard_map/all_to_all | solution.py:222
  10.5 0.0 copy-done.4
  10.5 0.0 copy-start.5
  10.5 3.1 %slice.50 = bf16[8,2,512,128]{3,2,1,0:T(8,128)(2,1)} slice(bf16[8,4,512,128]{3,2,1,0:T(8,128)(2,1)} %bitcast.53), slice={[0:8], [0:2], [0:512], [0:128]} | slice | bytes 4194304 | tf_op jit(solution)/shard_map/slice | solution.py:235
  13.7 0.0 copy-done.5
  13.7 0.1 slice_bitcast_fusion.11
  13.8 0.0 copy-start.3
  13.8 45.0 %all-to-all-done.obs_ref = bf16[8,2,512,128]{3,2,1,0:T(8,128)(2,1)S(1)} async-done(((bf16[8,2,512,128]{3,2,1,0:T(8,128)(2,1)}), bf16[8,2,512,128]{3,2,1,0:T(8,128)(2,1)S(1)}, u32[]{:S(2)}, u32[]{:S(2)}) %all-to-all-start) | async-done | bytes 2097184 | tf_op jit(solution)/shard_map/all_to_all | solution.py:222
  58.7 0.0 copy-start.1
  58.7 1.3 copy-done.1
  60.1 3.6 %all-to-all-start.1 = ((bf16[8,2,512,128]{3,2,1,0:T(8,128)(2,1)}), bf16[8,2,512,128]{3,2,1,0:T(8,128)(2,1)S(1)}, u32[]{:S(2)}, u32[]{:S(2)}) async-start(bf16[8,2,512,128]{3,2,1,0:T(8,128)(2,1)} %slice.50), calls=%async_computation.1 | async-start | bytes 4194304 | tf_op jit(solution)/shard_map/all_to_all | solution.py:222
  63.7 0.0 copy-done.3
  63.7 0.0 copy-start.2
  63.7 1.6 copy-done.2
  65.3 32.7 %shard_map.46 = bf16[2,16,256,128]{3,2,1,0:T(8,128)(2,1)S(1)} custom-call(s32[2]{0:T(128)S(1)} %get-tuple-element.20.counts_ref, bf16[8,2,512,128]{3,2,1,0:T(8,128)(2,1)S(1)} %copy-done.2, bf16[2,16,256]{2,1,0:T(8,128)(2,1)S(1)} %get-tuple-element.18.mask_ref, bf16[8,256,256]{2,1,0:T(8,128)(2,1)S(1)} %copy-done.3), custom_call_target="tpu_custom_call" | custom-call | flops 42949672960 | bytes 8388608 | tf_op jit(solution)/shard_map/pallas_call | solution.py:198
  98.0 0.0 copy-start
  98.0 0.9 slice_bitcast_fusion.4
  98.9 0.6 copy-done
  99.5 1.1 fusion.7
  100.6 11.5 %all-to-all-done.1.obs_ref = bf16[8,2,512,128]{3,2,1,0:T(8,128)(2,1)S(1)} async-done(((bf16[8,2,512,128]{3,2,1,0:T(8,128)(2,1)}), bf16[8,2,512,128]{3,2,1,0:T(8,128)(2,1)S(1)}, u32[]{:S(2)}, u32[]{:S(2)}) %all-to-all-start.1) | async-done | bytes 2097184 | tf_op jit(solution)/shard_map/all_to_all | solution.py:222
  112.1 4.2 %collective-permute-start = (bf16[8,256,128]{2,1,0:T(8,128)(2,1)}, bf16[8,256,128]{2,1,0:T(8,128)(2,1)}, u32[]{:S(2)}, u32[]{:S(2)}) collective-permute-start(bf16[8,256,128]{2,1,0:T(8,128)(2,1)} %slice_bitcast_fusion.4), channel_id=1, source_target_pairs={{0,4},{4,8},{8,12},{12,16},{16,20},{20,24},{24,28},{1,5},{5,9},{9,... | collective-permute-start | bytes 1572872 | tf_op jit(solution)/shard_map/ppermute | solution.py:218
  116.3 4.3 %all-to-all-start.3 = ((bf16[8,256,128]{2,1,0:T(8,128)(2,1)}), bf16[8,256,128]{2,1,0:T(8,128)(2,1)}, u32[]{:S(2)}, u32[]{:S(2)}) async-start(bf16[8,256,128]{2,1,0:T(8,128)(2,1)} %fusion.7), calls=%async_computation.3 | async-start | bytes 1048576 | tf_op jit(solution)/shard_map/all_to_all | solution.py:222
  120.6 32.7 %shard_map.47 = bf16[2,16,256,128]{3,2,1,0:T(8,128)(2,1)S(1)} custom-call(s32[2]{0:T(128)S(1)} %get-tuple-element.19.counts_ref, bf16[8,2,512,128]{3,2,1,0:T(8,128)(2,1)S(1)} %all-to-all-done.1.obs_ref, bf16[2,16,256]{2,1,0:T(8,128)(2,1)S(1)} %get-tuple-element.17.mask_ref, bf16[8,256,256]{2,1,0:T(8,128)(2,1)S(1)} %copy-done.3), custom_call_target="tpu_custom_call" | custom-call | flops 42949672960 | bytes 8388608 | tf_op jit(solution)/shard_map/pallas_call | solution.py:198
  153.3 1.5 fusion.3
  154.9 0.0 collective-permute-done
  154.9 1.3 fusion.8
  156.2 0.2 pad_maximum_fusion.1
  156.4 0.1 copy.6
  156.5 0.0 all-to-all-done.3
  156.5 39.7 %all_to_all.20 = bf16[8,3,256,128]{3,2,1,0:T(8,128)(2,1)S(1)} all-to-all(bf16[8,3,256,128]{3,2,1,0:T(8,128)(2,1)S(1)} %copy.6), channel_id=1, replica_groups=mesh['shot'=8,'az'=4] {'shot'}, dimensions={0} | all-to-all | bytes 3145728 | tf_op jit(solution)/shard_map/all_to_all | solution.py:222
  196.2 2.5 %pad_maximum_fusion = bf16[8,4,256,128]{3,2,1,0:T(8,128)(2,1)} fusion(bf16[8,1,256,128]{3,2,1,0:T(8,128)(2,1)} %bitcast.15, bf16[8,3,256,128]{3,2,1,0:T(8,128)(2,1)S(1)} %all_to_all.20), kind=kLoop, calls=%fused_computation | loop fusion | flops 1048576 | bytes 4194304 | tf_op jit(solution)/shard_map/concatenate | solution.py:258
  (3 shorter events, 0.0 us)
Async XLA Ops:
  3.1 7.4 %copy-start.4 = (s32[1,4,16,256]{3,2,1,0:T(8,128)S(1)}, s32[1,4,16,256]{3,2,1,0:T(8,128)}, u32[]{:S(2)}) copy-start(s32[1,4,16,256]{3,2,1,0:T(8,128)} %param.5) | copy-start | bytes 196612
  3.1 55.6 %all-to-all-start = ((bf16[8,2,512,128]{3,2,1,0:T(8,128)(2,1)}), bf16[8,2,512,128]{3,2,1,0:T(8,128)(2,1)S(1)}, u32[]{:S(2)}, u32[]{:S(2)}) async-start(bf16[8,2,512,128]{3,2,1,0:T(8,128)(2,1)} %slice.58), calls=%async_computation | async-start | bytes 4194304 | tf_op jit(solution)/shard_map/all_to_all | solution.py:222
  10.5 3.2 %copy-start.5 = (s32[1,4]{1,0:T(1,128)S(1)}, s32[1,4]{1,0:T(1,128)}, u32[]{:S(2)}) copy-start(s32[1,4]{1,0:T(1,128)} %param.6) | copy-start | bytes 52
  13.8 49.9 %copy-start.3 = (bf16[8,256,256]{2,1,0:T(8,128)(2,1)S(1)}, bf16[8,256,256]{2,1,0:T(8,128)(2,1)}, u32[]{:S(2)}) copy-start(bf16[8,256,256]{2,1,0:T(8,128)(2,1)} %constant.9.clone.table_ref) | copy-start | bytes 3145732
  58.7 1.3 copy-start.1
  60.1 52.1 %all-to-all-start.1 = ((bf16[8,2,512,128]{3,2,1,0:T(8,128)(2,1)}), bf16[8,2,512,128]{3,2,1,0:T(8,128)(2,1)S(1)}, u32[]{:S(2)}, u32[]{:S(2)}) async-start(bf16[8,2,512,128]{3,2,1,0:T(8,128)(2,1)} %slice.50), calls=%async_computation.1 | async-start | bytes 4194304 | tf_op jit(solution)/shard_map/all_to_all | solution.py:222
  63.7 1.6 copy-start.2
  98.0 1.5 copy-start
  112.1 42.8 %collective-permute-start = (bf16[8,256,128]{2,1,0:T(8,128)(2,1)}, bf16[8,256,128]{2,1,0:T(8,128)(2,1)}, u32[]{:S(2)}, u32[]{:S(2)}) collective-permute-start(bf16[8,256,128]{2,1,0:T(8,128)(2,1)} %slice_bitcast_fusion.4), channel_id=1, source_target_pairs={{0,4},{4,8},{8,12},{12,16},{16,20},{20,24},{24,28},{1,5},{5,9},{9,... | collective-permute-start | bytes 1572872 | tf_op jit(solution)/shard_map/ppermute | solution.py:218
  116.3 40.2 %all-to-all-start.3 = ((bf16[8,256,128]{2,1,0:T(8,128)(2,1)}), bf16[8,256,128]{2,1,0:T(8,128)(2,1)}, u32[]{:S(2)}, u32[]{:S(2)}) async-start(bf16[8,256,128]{2,1,0:T(8,128)(2,1)} %fusion.7), calls=%async_computation.3 | async-start | bytes 1048576 | tf_op jit(solution)/shard_map/all_to_all | solution.py:222
